TPU v7x, 32 devices: a whole 2x2x4 slice. The times are simulated.
32 devices in a mesh: parts: 2 (over x), expert: 16 (over z, y, core).
Axes of the slice: x: 2, y: 2, z: 4, core: 2. Of those that a mesh axis runs over, the one named last changes fastest.
Arguments:
- hidden: bfloat16 [512, 2048], P(('parts', 'expert')), parts along dimension 0, may hold values from -6 to 6
- parent: int32 [512], P(('parts', 'expert')), parts along dimension 0, may hold values from 0 to 255, as said below
- expert_ids: int32 [512, 8], P(('parts', 'expert')), parts along dimension 0, may hold values from 0 to 15, all different within a row; in each aligned block of 16 rows (0 to 15, 16 to 31, ...) at most 16 rows name the same one
- route_weight: float32 [512, 8], P(('parts', 'expert')), parts along dimension 0, may hold values from 0.05 to 1
- norm_gain: float32 [2048], replicated, may hold values from 0.1 to 1.9
- w_gate: bfloat16 [16, 2048, 768], P('expert'), may hold values from -0.125 to 0.125
- w_up: bfloat16 [16, 2048, 768], P('expert'), may hold values from -0.125 to 0.125
- w_down: bfloat16 [16, 768, 2048], P('expert'), may hold values from -0.21875 to 0.21875
Outputs:
- layer_out: bfloat16 [512, 2048], P(('parts', 'expert')), parts along dimension 0
There are 2 independent parts, one for each index of `parts`. A program takes and returns all parts, laid end to end along the dimension named above; an argument that names none is the same for every part. Nothing has to cross between parts.
Inputs may be any that keep to these rules, and one draw needn't show every extreme that they name: The parent of a row among the rows 16 * i to 16 * i + 15 lies in the same range or in the range just before it. `expert_ids`: in each aligned block of 16 rows (the rows of one device) no expert is named by more than 16 rows, a bound that some block reaches.
All inputs are finite; a program needn't handle non-finite values.
Results may differ from a plain program's by a relative error of at most 0.0033.
Values may be sent and summed in bfloat16 or wider, within the bound.
A program may use at most 64 MiB of HBM per device.

v0:
```python
import jax
import jax.numpy as jnp
from jax import lax
from jax.sharding import PartitionSpec as P


def shifted(shard, axis, by):
    peers = lax.axis_size(axis)
    pairs = [(i, i + by) for i in range(peers) if 0 <= i + by < peers]
    return lax.ppermute(shard, axis, pairs)


def per_device(hidden, parent, expert_ids, route_weight, norm_gain, w_gate, w_up, w_down):
    row_count = hidden.shape[0]
    width = hidden.shape[1]
    route_count = expert_ids.shape[1]
    expert_count = lax.axis_size("expert")
    capacity = 2 * row_count * route_count // expert_count
    my_index = lax.axis_index("expert")
    first_row = my_index * row_count
    before = shifted(hidden, "expert", 1)
    pool = jnp.concatenate([before, hidden], axis=0)
    local_parent = parent - (first_row - row_count)
    forked = jnp.take(pool, local_parent, axis=0)
    forked_f = forked.astype(jnp.float32)
    scale_row = lax.rsqrt(jnp.mean(forked_f * forked_f, axis=-1, keepdims=True) + 1e-06)
    normed = (forked_f * scale_row * norm_gain).astype(jnp.bfloat16)
    share = route_weight / jnp.sum(route_weight, axis=-1, keepdims=True)
    flat_ids = expert_ids.reshape(-1)
    expert_range = jnp.arange(expert_count, dtype=jnp.int32)
    onehot = (flat_ids[:, None] == expert_range[None, :]).astype(jnp.int32)
    earlier = jnp.cumsum(onehot, axis=0) - onehot
    slot_no = jnp.sum(earlier * onehot, axis=1)
    target = flat_ids * capacity + slot_no
    slot_range = jnp.arange(expert_count * capacity, dtype=jnp.int32)
    placing = (target[None, :] == slot_range[:, None]).astype(jnp.bfloat16)
    repeated = jnp.repeat(normed, route_count, axis=0)
    outgoing = jnp.dot(placing, repeated, preferred_element_type=jnp.float32).astype(jnp.bfloat16)
    outgoing = outgoing.reshape(expert_count, capacity, width)
    block = lax.all_to_all(outgoing, "expert", split_axis=0, concat_axis=0, tiled=True)
    sources = block.shape[0]
    items = block.shape[1]
    inputs = block.reshape(sources * items, width)
    gate_val = jnp.dot(inputs, w_gate[0], preferred_element_type=jnp.float32)
    up_val = jnp.dot(inputs, w_up[0], preferred_element_type=jnp.float32)
    inner = (jax.nn.silu(gate_val) * up_val).astype(jnp.bfloat16)
    result = jnp.dot(inner, w_down[0], preferred_element_type=jnp.float32).astype(jnp.bfloat16)
    result = result.reshape(sources, items, width)
    returned = lax.all_to_all(result, "expert", split_axis=0, concat_axis=0, tiled=True)
    back_flat = returned.reshape(expert_count * capacity, width).astype(jnp.float32)
    target_rows = target.reshape(row_count, route_count)
    combining = jnp.sum(
        (target_rows[:, :, None] == slot_range[None, None, :]).astype(jnp.float32)
        * share[:, :, None],
        axis=1,
    )
    mixed = jnp.dot(
        combining, back_flat, precision=lax.Precision.HIGHEST, preferred_element_type=jnp.float32
    )
    return (forked_f + mixed).astype(jnp.bfloat16)


def solution(mesh):
    in_specs = (
        P(("parts", "expert"), None),
        P(("parts", "expert")),
        P(("parts", "expert"), None),
        P(("parts", "expert"), None),
        P(),
        P("expert", None, None),
        P("expert", None, None),
        P("expert", None, None),
    )
    out_specs = P(("parts", "expert"), None)
    return jax.shard_map(
        per_device, mesh=mesh, in_specs=in_specs, out_specs=out_specs, check_vma=False
    )
```

profile of v0, /device:TPU:0, one launch (start us, length us, event | category | flops | bytes accessed | tf_op | source)
XLA Modules:
  0.0 80.0 jit_solution(4912489347025923295)
XLA Ops:
  0.0 0.0 copy-start
  0.0 2.6 %collective-permute-start = (bf16[16,2048]{1,0:T(8,128)(2,1)}, bf16[16,2048]{1,0:T(8,128)(2,1)S(1)}, u32[]{:S(2)}, u32[]{:S(2)}) collective-permute-start(bf16[16,2048]{1,0:T(8,128)(2,1)} %param.8), channel_id=1, source_target_pairs={{0,1},{1,2},{2,3},{3,4},{4,5},{5,6},{6,7},{7,8},{8,9},{9,10},{10,1... | collective-permute-start | bytes 196616 | tf_op jit(solution)/shard_map/ppermute | solution.py:10
  2.6 0.8 copy.15
  3.4 0.1 eq.20
  3.5 0.1 fusion.25
  3.6 0.2 reduce_window_sum.11
  3.7 0.2 select_reduce_fusion.1
  3.9 0.7 compare_and_fusion
  4.6 0.0 collective-permute-done
  4.6 0.9 %pad_maximum_fusion = bf16[32,2048]{1,0:T(8,128)(2,1)S(1)} fusion(bf16[16,2048]{1,0:T(8,128)(2,1)} %param.8, bf16[16,2048]{1,0:T(8,128)(2,1)S(1)} %collective-permute-done), kind=kLoop, calls=%fused_computation.21 | loop fusion | flops 262144 | bytes 262144 | tf_op jit(solution)/shard_map/concatenate | solution.py:22
  5.5 0.6 gather_fusion
  6.1 0.0 copy-start.3
  6.1 0.2 fusion.21
  6.3 0.9 %fusion.23 = bf16[16,2048]{1,0:T(8,128)(2,1)S(1)} fusion(f32[2048]{0:T(1024)} %param.12, f32[16]{0:T(128)S(1)} %add_rsqrt_fusion, bf16[16,2048]{1,0:T(8,128)(2,1)S(1)} %gather_fusion, pred[16]{0:T(512)(128)(4,1)S(1)} %get-tuple-element.5), kind=kLoop, calls=%fused_computation.20 | loop fusion | flops 163840 | bytes 139344 | tf_op jit(solution)/shard_map/convert_element_type | solution.py:27
  7.2 0.4 convolution_convert_fusion
  7.7 33.5 %all_to_all.10 = bf16[16,16,2048]{2,1,0:T(8,128)(2,1)S(1)} all-to-all(bf16[16,16,2048]{2,1,0:T(8,128)(2,1)S(1)} %bitcast.28), channel_id=1, replica_groups=mesh['parts'=2,'expert'=16] {'expert'}, dimensions={0} | all-to-all | bytes 2097152 | tf_op jit(solution)/shard_map/all_to_all | solution.py:40
  41.1 0.0 copy-start.1
  41.1 1.0 %copy-done.1 = bf16[16,16,2048]{2,1,0:T(8,128)(2,1)} copy-done((bf16[16,16,2048]{2,1,0:T(8,128)(2,1)}, bf16[16,16,2048]{2,1,0:T(8,128)(2,1)S(1)}, u32[]{:S(2)}) %copy-start.1) | copy-done | bytes 1048600
  42.2 0.0 copy-done.3
  42.2 1.9 %fusion.4 = f32[256,768]{1,0:T(8,128)} fusion(bf16[256,2048]{1,0:T(8,128)(2,1)S(1)} %bitcast.30, bf16[1,2048,768]{2,1,0:T(8,128)(2,1)S(1)} %copy-done.3), kind=kOutput, calls=%fused_computation.5 | convolution fusion | flops 805306368 | bytes 4980736 | tf_op jit(solution)/shard_map/dot_general | solution.py:44
  44.1 0.0 copy-done
  44.1 0.0 copy-start.2
  44.1 5.5 %fusion.6 = bf16[256,2048]{1,0:T(8,128)(2,1)} fusion(bf16[1,768,2048]{2,1,0:T(8,128)(2,1)S(1)} %copy-done, bf16[256,2048]{1,0:T(8,128)(2,1)} %bitcast.31, bf16[1,2048,768]{2,1,0:T(8,128)(2,1)} %param.14, f32[256,768]{1,0:T(8,128)} %fusion.4), kind=kOutput, calls=%fused_computation.8 | convolution fusion | flops 1612316672 | bytes 9175040 | tf_op jit(solution)/shard_map/dot_general | solution.py:47
  49.6 5.0 %all-to-all-start.1 = ((bf16[16,16,2048]{2,1,0:T(8,128)(2,1)}), bf16[16,16,2048]{2,1,0:T(8,128)(2,1)}, u32[]{:S(2)}, u32[]{:S(2)}) async-start(bf16[16,16,2048]{2,1,0:T(8,128)(2,1)} %bitcast.29), calls=%async_computation.1 | async-start | bytes 2097152 | tf_op jit(solution)/shard_map/all_to_all | solution.py:49
  54.6 0.1 reduce_sum.39
  54.7 0.0 copy-done.2
  54.8 0.1 copy.17
  54.8 0.1 select_reduce_fusion
  55.0 22.7 %all-to-all-done.1 = bf16[16,16,2048]{2,1,0:T(8,128)(2,1)} async-done(((bf16[16,16,2048]{2,1,0:T(8,128)(2,1)}), bf16[16,16,2048]{2,1,0:T(8,128)(2,1)}, u32[]{:S(2)}, u32[]{:S(2)}) %all-to-all-start.1) | async-done | bytes 1048608 | tf_op jit(solution)/shard_map/all_to_all | solution.py:49
  77.6 2.4 %fusion.9 = bf16[16,2048]{1,0:T(8,128)(2,1)} fusion(f32[16,256]{1,0:T(8,128)S(1)} %select_reduce_fusion, bf16[256,2048]{1,0:T(8,128)(2,1)} %bitcast.7, bf16[16,2048]{1,0:T(8,128)(2,1)S(1)} %gather_fusion, pred[16]{0:T(512)(128)(4,1)S(1)} %get-tuple-element.5), kind=kOutput, calls=%fused_computation.10 | convolution fusion | flops 100794368 | bytes 1196048 | tf_op jit(solution)/shard_map/dot_general | solution.py:57
  (6 shorter events, 0.1 us)
Async XLA Ops:
  0.0 44.1 %copy-start = (bf16[1,768,2048]{2,1,0:T(8,128)(2,1)S(1)}, bf16[1,768,2048]{2,1,0:T(8,128)(2,1)}, u32[]{:S(2)}) copy-start(bf16[1,768,2048]{2,1,0:T(8,128)(2,1)} %param.15) | copy-start | bytes 9437188
  0.0 4.6 %collective-permute-start = (bf16[16,2048]{1,0:T(8,128)(2,1)}, bf16[16,2048]{1,0:T(8,128)(2,1)S(1)}, u32[]{:S(2)}, u32[]{:S(2)}) collective-permute-start(bf16[16,2048]{1,0:T(8,128)(2,1)} %param.8), channel_id=1, source_target_pairs={{0,1},{1,2},{2,3},{3,4},{4,5},{5,6},{6,7},{7,8},{8,9},{9,10},{10,1... | collective-permute-start | bytes 196616 | tf_op jit(solution)/shard_map/ppermute | solution.py:10
  6.1 36.1 %copy-start.3 = (bf16[1,2048,768]{2,1,0:T(8,128)(2,1)S(1)}, bf16[1,2048,768]{2,1,0:T(8,128)(2,1)}, u32[]{:S(2)}) copy-start(bf16[1,2048,768]{2,1,0:T(8,128)(2,1)} %param.13) | copy-start | bytes 9437188
  41.1 1.0 %copy-start.1 = (bf16[16,16,2048]{2,1,0:T(8,128)(2,1)}, bf16[16,16,2048]{2,1,0:T(8,128)(2,1)S(1)}, u32[]{:S(2)}) copy-start(bf16[16,16,2048]{2,1,0:T(8,128)(2,1)S(1)} %all_to_all.10) | copy-start | bytes 3145732
  44.1 10.7 %copy-start.2 = (f32[16,8]{0,1:T(8,128)S(1)}, f32[16,8]{0,1:T(8,128)}, u32[]{:S(2)}) copy-start(f32[16,8]{0,1:T(8,128)} %param.11) | copy-start | bytes 1540
  49.6 28.0 %all-to-all-start.1 = ((bf16[16,16,2048]{2,1,0:T(8,128)(2,1)}), bf16[16,16,2048]{2,1,0:T(8,128)(2,1)}, u32[]{:S(2)}, u32[]{:S(2)}) async-start(bf16[16,16,2048]{2,1,0:T(8,128)(2,1)} %bitcast.29), calls=%async_computation.1 | async-start | bytes 2097152 | tf_op jit(solution)/shard_map/all_to_all | solution.py:49
where the time goes:
time: 81.5 us; the launch traced here: 80 us
  blocking collectives  33.5 us (41%)
  waiting for transfers between devices  22.7 us (28%)
  matrix products  10.2 us (13%)
  starting transfers between devices  7.66 us (9%)
  other arithmetic  3.27 us (4%)
  local copies, waits for them, and re-layouts  2.65 us (3%)
    all_to_all x1, blocking collectives, per_device(): lax.all_to_all(outgoing, 'expert', split_axis=0, concat_axis=0, tiled=True)  33.5 us
    all_to_all x1, waiting for transfers between devices, per_device(): lax.all_to_all(result, 'expert', split_axis=0, concat_axis=0, tiled=True)  22.7 us
    dot_general x1, matrix products, per_device(): jnp.dot(inner, w_down[0], preferred_element_type=jnp.float32)  5.52 us
    all_to_all x1, starting transfers between devices, per_device(): lax.all_to_all(result, 'expert', split_axis=0, concat_axis=0, tiled=True)  5.05 us
    ppermute x1, starting transfers between devices, shifted(): return lax.ppermute(shard, axis, pairs)  2.61 us
    dot_general x1, matrix products, per_device(): jnp.dot(combining, back_flat, precision=lax.Precision.HIGHEST, preferred_...  2.38 us
    dot_general x1, matrix products, per_device(): gate_val = jnp.dot(inputs, w_gate[0], preferred_element_type=jnp.float32)  1.9 us
    unnamed x9, local copies, waits for them, and re-layouts  1.81 us
  transfers between devices with their start and end apart: 2, of which 1 were waited for; matrix products, arithmetic and copies ran while one was open for 3% of the time, Pallas kernels for 0%

commit v1 on v0

--- a/solution.py
+++ b/solution.py
@@ -1,7 +1,286 @@
+import functools
+
 import jax
 import jax.numpy as jnp
 from jax import lax
+from jax.experimental import pallas as pl
+from jax.experimental.pallas import tpu as pltpu
 from jax.sharding import PartitionSpec as P
+
+MESH = pl.DeviceIdType.MESH
+GATHER_CHUNKS = 2
+RETURN_CHUNKS = 2
+LANES = 128
+
+
+def dense_kernel(
+    parent_ref, hidden_ref, ids_ref, weight_ref, gain_ref, gate_hbm, up_hbm, down_hbm,
+    out_ref,
+    *scratch,
+    experts, zs,
+):
+    gc, rc = GATHER_CHUNKS, RETURN_CHUNKS
+    scratch = list(scratch)
+    rows_in = [scratch.pop(0) for _ in range(gc)]
+    (gate_w, up_w, down_w, gate_acc, up_acc, inner, forked_inner, share_ref, prev,
+     kept, core_out, core_in, y_out, y_in, z_out, z_in,
+     w_sem, g_send, g_recv, r_send, r_recv, p_sem) = scratch
+    rows, width = hidden_ref.shape
+    hidden_units = gate_w.shape[1]
+    total = rows * experts
+    half = total // 2
+    quarter = total // 4
+    gw = width // gc
+    rw = width // rc
+    bits = zs.bit_length() - 1
+
+    w_copies = [
+        pltpu.make_async_copy(gate_hbm.at[0], gate_w, w_sem.at[0]),
+        pltpu.make_async_copy(up_hbm.at[0], up_w, w_sem.at[1]),
+        pltpu.make_async_copy(down_hbm.at[0], down_w, w_sem.at[2]),
+    ]
+    for copy in w_copies:
+        copy.start()
+
+    me = lax.axis_index("expert")
+    core = lax.rem(me, 2)
+    y = lax.rem(lax.div(me, 2), 2)
+    z_bits = [lax.rem(lax.div(me, 4 << b), 2) for b in range(bits)]
+
+    def flipped(dz, dy, dc):
+        index = (1 - core if dc else core) + 2 * (1 - y if dy else y)
+        for b in range(bits):
+            index = index + (4 << b) * (1 - z_bits[b] if (dz >> b) & 1 else z_bits[b])
+        return index
+
+    z_peers = [flipped(dz, 0, 0) for dz in range(zs)]
+    y_peer = flipped(0, 1, 0)
+    core_peer = flipped(0, 0, 1)
+    after = lax.rem(me + 1, experts)
+    before = lax.rem(me + experts - 1, experts)
+
+    barrier = pltpu.get_barrier_semaphore()
+    greeted = z_peers[1:] + [y_peer, core_peer, after, before]
+    for peer in greeted:
+        pl.semaphore_signal(barrier, inc=1, device_id={"expert": peer}, device_id_type=MESH)
+
+    own = hidden_ref[...].astype(jnp.float32)
+    scale = lax.rsqrt(jnp.mean(own * own, axis=-1, keepdims=True) + 1e-06)
+    normed = (own * scale * gain_ref[...]).astype(jnp.bfloat16)
+    row_no = lax.broadcasted_iota(jnp.int32, (rows, LANES), 0)
+    lane = lax.broadcasted_iota(jnp.int32, (rows, LANES), 1)
+    parents = jnp.zeros((rows, LANES), jnp.int32)
+    for r in range(rows):
+        parents = jnp.where(row_no == r, parent_ref[r], parents)
+    share = weight_ref[...] / jnp.sum(weight_ref[...], axis=-1, keepdims=True)
+    ids = ids_ref[...]
+    spread = jnp.zeros((rows, LANES), jnp.float32)
+    lane_expert = lax.rem(lane, experts)
+    for k in range(ids.shape[1]):
+        spread = spread + jnp.where(lane_expert == ids[:, k:k + 1], share[:, k:k + 1], 0.0)
+    high = spread.astype(jnp.bfloat16).astype(jnp.float32)
+    middle = (spread - high).astype(jnp.bfloat16).astype(jnp.float32)
+    low = spread - high - middle
+    meta = jnp.where(
+        lane < experts, high,
+        jnp.where(lane < 2 * experts, middle,
+                  jnp.where(lane < 3 * experts, low,
+                            jnp.where(lane == 3 * experts, parents.astype(jnp.float32), 0.0))))
+    for k in range(gc):
+        rows_in[k][0:rows, 0:gw] = normed[:, k * gw:(k + 1) * gw]
+    rows_in[0][0:rows, gw:gw + LANES] = meta.astype(jnp.bfloat16)
+
+    pl.semaphore_wait(barrier, len(greeted))
+
+    sends = []
+
+    def remote(src, dst, send, recv, peer):
+        return pltpu.make_async_remote_copy(
+            src_ref=src, dst_ref=dst, send_sem=send, recv_sem=recv,
+            device_id={"expert": peer}, device_id_type=MESH)
+
+    def gather(k, first, count, target, number, peer):
+        buf = rows_in[k]
+        return remote(buf.at[pl.ds(first * rows, count * rows), :],
+                      buf.at[pl.ds(target * rows, count * rows), :],
+                      g_send.at[k, number], g_recv.at[k, number], peer)
+
+    def go(copy):
+        copy.start()
+        sends.append(copy)
+        return copy
+
+    z_copies, y_copies, c_copies = [], [], []
+    for k in range(gc):
+        z_copies.append([go(gather(k, 0, 1, dz, dz - 1, z_peers[dz])) for dz in range(1, zs)])
+        y_copies.append([go(gather(k, 0, 1, zs, zs, y_peer))])
+        c_copies.append([go(gather(k, 0, 1, 2 * zs, zs + 1, core_peer))])
+    before_copy = None
+    tile = 256
+    for step in range(gc + 2):
+        k = step
+        if k < gc:
+            for copy in z_copies[k]:
+                copy.wait_recv()
+            y_copies[k].append(go(gather(k, 1, zs - 1, zs + 1, zs + 2, y_peer)))
+            c_copies[k].append(go(gather(k, 1, zs - 1, 2 * zs + 1, zs + 3, core_peer)))
+        k = step - 1
+        if 0 <= k < gc:
+            for copy in y_copies[k]:
+                copy.wait_recv()
+            c_copies[k].append(go(gather(k, zs, zs, 3 * zs, zs + 4, core_peer)))
+        k = step - 2
+        if 0 <= k < gc:
+            for copy in c_copies[k]:
+                copy.wait_recv()
+            if k == 0:
+                w_copies[0].wait()
+                w_copies[1].wait()
+            if k == gc - 1:
+                before_copy = go(remote(hidden_ref, prev, p_sem.at[0], p_sem.at[1], after))
+
+            @pl.loop(0, hidden_units // tile)
+            def _(t):
+                columns = pl.ds(pl.multiple_of(t * tile, tile), tile)
+                block = rows_in[k][:, 0:gw]
+                gate = jnp.dot(block, gate_w[k * gw:(k + 1) * gw, columns],
+                               preferred_element_type=jnp.float32)
+                up = jnp.dot(block, up_w[k * gw:(k + 1) * gw, columns],
+                             preferred_element_type=jnp.float32)
+                if k > 0:
+                    gate = gate + gate_acc[:, columns]
+                    up = up + up_acc[:, columns]
+                if k < gc - 1:
+                    gate_acc[:, columns] = gate
+                    up_acc[:, columns] = up
+                else:
+                    inner[:, columns] = (gate / (1.0 + jnp.exp(-gate)) * up).astype(jnp.bfloat16)
+
+            if k == 0:
+                facts = rows_in[0][:, gw:gw + LANES].astype(jnp.float32)
+                lanes = lax.broadcasted_iota(jnp.int32, (total, LANES), 1)
+                mine = (lax.rem(lanes, experts) == me) & (lanes < 3 * experts)
+                share_ref[...] = jnp.sum(jnp.where(mine, facts, 0.0), axis=1, keepdims=True)
+                wanted = facts[:, 3 * experts:3 * experts + 1]
+                held = lax.broadcasted_iota(jnp.int32, (total, total), 1)
+                slot = lax.div(held, rows)
+                dz = lax.rem(slot, zs)
+                dy = lax.rem(lax.div(slot, zs), 2)
+                dc = lax.div(slot, 2 * zs)
+                owner = dc + core - 2 * core * dc + 2 * (dy + y - 2 * y * dy)
+                for b in range(bits):
+                    bit = lax.rem(lax.div(dz, 1 << b), 2)
+                    owner = owner + (4 << b) * (bit + z_bits[b] - 2 * z_bits[b] * bit)
+                at = (owner * rows + lax.rem(held, rows)).astype(jnp.float32)
+                choose = jnp.where(at == wanted, 1.0, 0.0).astype(jnp.bfloat16)
+
+    forked_inner[...] = jnp.dot(
+        choose, inner[...], preferred_element_type=jnp.float32).astype(jnp.bfloat16)
+    w_copies[2].wait()
+    core_copies = []
+    for k in range(rc):
+
+        @pl.loop(0, rw // tile)
+        def _(t):
+            columns = pl.ds(pl.multiple_of(k * rw + t * tile, tile), tile)
+            local = pl.ds(pl.multiple_of(t * tile, tile), tile)
+            result = jnp.dot(forked_inner[...], down_w[:, columns],
+                             preferred_element_type=jnp.float32)
+            result = result.astype(jnp.bfloat16).astype(jnp.float32) * share_ref[...]
+            kept[k, :, local] = result[0:half]
+            core_out[k, :, local] = result[half:total].astype(jnp.bfloat16)
+
+        core_copies.append(go(remote(core_out.at[k], core_in.at[k],
+                                     r_send.at[k, 0], r_recv.at[k, 0], core_peer)))
+
+    y_back = []
+    for k in range(rc):
+        core_copies[k].wait_recv()
+        y_out[k] = (kept[k, quarter:half] + core_in[k, quarter:half].astype(jnp.float32)
+                    ).astype(jnp.bfloat16)
+        y_back.append(go(remote(y_out.at[k], y_in.at[k],
+                                r_send.at[k, 1], r_recv.at[k, 1], y_peer)))
+
+    before_copy.wait_recv()
+    pool_no = lax.broadcasted_iota(jnp.int32, (rows, 2 * rows), 1)
+    pick = jnp.where(parents[:, 0:2 * rows] - (me - 1) * rows == pool_no, 1.0, 0.0)
+    pick = pick.astype(jnp.bfloat16)
+
+    z_back = []
+    for k in range(rc):
+        y_back[k].wait_recv()
+        summed = (kept[k, 0:quarter] + core_in[k, 0:quarter].astype(jnp.float32)
+                  + y_in[k].astype(jnp.float32))
+        kept[k, 0:rows] = summed[0:rows]
+        z_out[k] = summed[rows:quarter].astype(jnp.bfloat16)
+        z_back.append([
+            go(remote(z_out.at[k, pl.ds((dz - 1) * rows, rows), :],
+                      z_in.at[k, pl.ds((dz - 1) * rows, rows), :],
+                      r_send.at[k, 1 + dz], r_recv.at[k, 1 + dz], z_peers[dz]))
+            for dz in range(1, zs)])
+
+    for k in range(rc):
+        columns = slice(k * rw, (k + 1) * rw)
+        forked = (
+            jnp.dot(pick[:, 0:rows], prev[:, columns], preferred_element_type=jnp.float32)
+            + jnp.dot(pick[:, rows:2 * rows], hidden_ref[:, columns],
+                      preferred_element_type=jnp.float32))
+        mixed = kept[k, 0:rows]
+        for dz in range(1, zs):
+            z_back[k][dz - 1].wait_recv()
+            mixed = mixed + z_in[k, (dz - 1) * rows:dz * rows].astype(jnp.float32)
+        out_ref[:, columns] = (forked + mixed).astype(out_ref.dtype)
+
+    for copy in sends:
+        copy.wait_send()
+
+
+def dense(hidden, parent, expert_ids, route_weight, norm_gain, w_gate, w_up, w_down):
+    rows, width = hidden.shape
+    experts = lax.axis_size("expert")
+    zs = experts // 4
+    units = w_gate.shape[2]
+    total = rows * experts
+    gc, rc = GATHER_CHUNKS, RETURN_CHUNKS
+    gw, rw = width // gc, width // rc
+    bf16, f32 = jnp.bfloat16, jnp.float32
+    vmem = pl.BlockSpec(memory_space=pltpu.VMEM)
+    hbm = pl.BlockSpec(memory_space=pl.ANY)
+    return pl.pallas_call(
+        functools.partial(dense_kernel, experts=experts, zs=zs),
+        out_shape=jax.ShapeDtypeStruct((rows, width), hidden.dtype),
+        in_specs=[pl.BlockSpec(memory_space=pltpu.SMEM), vmem, vmem, vmem, vmem, hbm, hbm, hbm],
+        out_specs=vmem,
+        scratch_shapes=[
+            pltpu.VMEM((total, gw + (LANES if k == 0 else 0)), bf16) for k in range(gc)
+        ] + [
+            pltpu.VMEM((width, units), bf16),
+            pltpu.VMEM((width, units), bf16),
+            pltpu.VMEM((units, width), bf16),
+            pltpu.VMEM((total, units), f32),
+            pltpu.VMEM((total, units), f32),
+            pltpu.VMEM((total, units), bf16),
+            pltpu.VMEM((total, units), bf16),
+            pltpu.VMEM((total, 1), f32),
+            pltpu.VMEM((rows, width), bf16),
+            pltpu.VMEM((rc, total // 2, rw), f32),
+            pltpu.VMEM((rc, total // 2, rw), bf16),
+            pltpu.VMEM((rc, total // 2, rw), bf16),
+            pltpu.VMEM((rc, total // 4, rw), bf16),
+            pltpu.VMEM((rc, total // 4, rw), bf16),
+            pltpu.VMEM((rc, total // 4 - rows, rw), bf16),
+            pltpu.VMEM((rc, total // 4 - rows, rw), bf16),
+            pltpu.SemaphoreType.DMA((3,)),
+            pltpu.SemaphoreType.DMA((gc, zs + 5)),
+            pltpu.SemaphoreType.DMA((gc, zs + 5)),
+            pltpu.SemaphoreType.DMA((rc, zs + 1)),
+            pltpu.SemaphoreType.DMA((rc, zs + 1)),
+            pltpu.SemaphoreType.DMA((2,)),
+        ],
+        compiler_params=pltpu.CompilerParams(
+            collective_id=0, has_side_effects=True, vmem_limit_bytes=48 * 1024 * 1024),
+    )(parent, hidden, expert_ids, route_weight, norm_gain.reshape(1, width),
+      w_gate, w_up, w_down)
 
 
 def shifted(shard, axis, by):
@@ -10,7 +289,7 @@
     return lax.ppermute(shard, axis, pairs)
 
 
-def per_device(hidden, parent, expert_ids, route_weight, norm_gain, w_gate, w_up, w_down):
+def routed(hidden, parent, expert_ids, route_weight, norm_gain, w_gate, w_up, w_down):
     row_count = hidden.shape[0]
     width = hidden.shape[1]
     route_count = expert_ids.shape[1]
@@ -60,6 +339,15 @@
     return (forked_f + mixed).astype(jnp.bfloat16)
 
 
+def per_device(hidden, *others):
+    experts = lax.axis_size("expert")
+    slots = 2 * hidden.shape[0] * others[1].shape[1]
+    fits = hidden.shape[0] * experts <= min(slots, 256) and 3 * experts < LANES
+    if fits and experts >= 8 and experts & (experts - 1) == 0:
+        return dense(hidden, *others)
+    return routed(hidden, *others)
+
+
 def solution(mesh):
     in_specs = (
         P(("parts", "expert"), None),

time: 81.5 us -> 41.7 us (0.51); the launches traced: 80 us -> 41.4 us
  Pallas kernels: 0 us -> 35.1 us
  blocking collectives: 33.5 us -> 0 us
  waiting for transfers between devices: 22.7 us -> 0 us
  matrix products: 10.2 us -> 0 us
  starting transfers between devices: 7.66 us -> 0 us
  local copies, waits for them, and re-layouts: 2.65 us -> 6.22 us
  other arithmetic: 3.27 us -> 0 us
    pallas_call x0 -> x1, Pallas kernels: none -> 35.1 us  [dense(): pl.pallas_call(functools.partial(dense_kernel, experts=experts, zs=zs), o...]
    all_to_all x1 -> x0, blocking collectives: 33.5 us -> none  [per_device(): lax.all_to_all(outgoing, 'expert', split_axis=0, concat_axis=0, tiled=True)]
    all_to_all x1 -> x0, waiting for transfers between devices: 22.7 us -> none  [per_device(): lax.all_to_all(result, 'expert', split_axis=0, concat_axis=0, tiled=True)]
    dot_general x4 -> x0, matrix products: 10.2 us -> none  [the longest x1 5.52 us: per_device(): jnp.dot(inner, w_down[0], preferred_element_type=jnp.float32)]
    all_to_all x1 -> x0, starting transfers between devices: 5.05 us -> none  [per_device(): lax.all_to_all(result, 'expert', split_axis=0, concat_axis=0, tiled=True)]
    unnamed x9 -> x11, local copies, waits for them, and re-layouts: 1.81 us -> 6.22 us
    ppermute x1 -> x0, starting transfers between devices: 2.61 us -> none  [shifted(): return lax.ppermute(shard, axis, pairs)]
    convert_element_type x2 -> x0, other arithmetic: 1.03 us -> none  [the longest x1 0.94 us: per_device(): normed = (forked_f * scale_row * norm_gain).astype(jnp.bfloat16)]
  transfers between devices with their start and end apart: 2 -> 0, of which waited for: 1 -> 0; matrix products, arithmetic and copies ran while one was open for 3% -> 0% of each run, Pallas kernels for 0% -> 0%
where the time goes in v1:
time: 41.7 us; the launch traced here: 41.4 us
  Pallas kernels  35.1 us (84%)
  local copies, waits for them, and re-layouts  6.22 us (15%)
    pallas_call x1, Pallas kernels, dense(): pl.pallas_call(functools.partial(dense_kernel, experts=experts, zs=zs), o...  35.1 us
    unnamed x11, local copies, waits for them, and re-layouts  6.22 us

profile of v1, /device:TPU:0, one launch (start us, length us, event | category | flops | bytes accessed | tf_op | source)
XLA Modules:
  0.0 41.4 jit_solution(12888504315428865851)
XLA Ops:
  0.0 0.8 %copy.9.ids_ref = s32[16,8]{1,0:T(8,128)S(1)} copy(s32[16,8]{0,1:T(8,128)} %param.10) | data formatting | bytes 1024 | tf_op args[2]
  0.8 0.8 %copy.10.weight_ref = f32[16,8]{1,0:T(8,128)S(1)} copy(f32[16,8]{0,1:T(8,128)} %param.11) | data formatting | bytes 1024 | tf_op args[3]
  1.5 0.0 copy-start
  1.5 1.9 %copy-done = bf16[1,2048,768]{2,1,0:T(8,128)(2,1)S(1)} copy-done((bf16[1,2048,768]{2,1,0:T(8,128)(2,1)S(1)}, bf16[1,2048,768]{2,1,0:T(8,128)(2,1)}, u32[]{:S(2)}) %copy-start) | copy-done | bytes 3145752
  3.4 0.0 copy-start.1
  3.4 0.8 %copy-done.1 = bf16[16,2048]{1,0:T(8,128)(2,1)S(1)} copy-done((bf16[16,2048]{1,0:T(8,128)(2,1)S(1)}, bf16[16,2048]{1,0:T(8,128)(2,1)}, u32[]{:S(2)}) %copy-start.1) | copy-done | bytes 65560
  4.2 0.0 copy-start.2
  4.2 0.7 %copy-done.2 = f32[2048]{0:T(1024)S(1)} copy-done((f32[2048]{0:T(1024)S(1)}, f32[2048]{0:T(1024)}, u32[]{:S(2)}) %copy-start.2) | copy-done | bytes 8216
  4.9 0.0 copy-start.3
  4.9 0.7 %copy-done.3 = s32[16]{0:T(128)S(1)} copy-done((s32[16]{0:T(128)S(1)}, s32[16]{0:T(128)}, u32[]{:S(2)}) %copy-start.3) | copy-done | bytes 88
  5.6 35.1 %shard_map.82 = bf16[16,2048]{1,0:T(8,128)(2,1)S(1)} custom-call(s32[16]{0:T(128)S(1)} %copy-done.3, bf16[16,2048]{1,0:T(8,128)(2,1)S(1)} %copy-done.1, s32[16,8]{1,0:T(8,128)S(1)} %copy.9.ids_ref, f32[16,8]{1,0:T(8,128)S(1)} %copy.10.weight_ref, f32[1,2048]{1,0:T(1,128)S(1)} %bitcast.1, bf16[1,2048,768]{2,1,0:T(8,128)(2,1)S(1)} %copy-done, ...), custom_call_target="tpu_custom_call" | custom-call | tf_op jit(solution)/shard_map/pallas_call | solution.py:249
  40.7 0.6 %copy.12 = bf16[16,2048]{1,0:T(8,128)(2,1)} copy(bf16[16,2048]{1,0:T(8,128)(2,1)S(1)} %shard_map.82) | data formatting | bytes 131072
Async XLA Ops:
  1.5 1.9 %copy-start = (bf16[1,2048,768]{2,1,0:T(8,128)(2,1)S(1)}, bf16[1,2048,768]{2,1,0:T(8,128)(2,1)}, u32[]{:S(2)}) copy-start(bf16[1,2048,768]{2,1,0:T(8,128)(2,1)} %gate_hbm.1) | copy-start | bytes 9437188
  3.4 0.8 %copy-start.1 = (bf16[16,2048]{1,0:T(8,128)(2,1)S(1)}, bf16[16,2048]{1,0:T(8,128)(2,1)}, u32[]{:S(2)}) copy-start(bf16[16,2048]{1,0:T(8,128)(2,1)} %hidden_ref.1) | copy-start | bytes 196612
  4.2 0.7 %copy-start.2 = (f32[2048]{0:T(1024)S(1)}, f32[2048]{0:T(1024)}, u32[]{:S(2)}) copy-start(f32[2048]{0:T(1024)} %param.12) | copy-start | bytes 24580
  4.9 0.7 %copy-start.3 = (s32[16]{0:T(128)S(1)}, s32[16]{0:T(128)}, u32[]{:S(2)}) copy-start(s32[16]{0:T(128)} %parent_ref.1) | copy-start | bytes 196

commit v2 on v1

--- a/solution.py
+++ b/solution.py
@@ -8,13 +8,25 @@
 from jax.sharding import PartitionSpec as P
 
 MESH = pl.DeviceIdType.MESH
-GATHER_CHUNKS = 2
+GATHER_CHUNKS = 1
 RETURN_CHUNKS = 2
 LANES = 128
 
 
+def gather_order(chunks, zs):
+    order, left = [], []
+    for k in range(chunks):
+        for dz in range(1, zs):
+            order.append(("z", k, dz))
+            if left:
+                order.append(left.pop(0))
+        order += left
+        left = [("y", k, dz) for dz in range(zs)] + [("c", k, 0)]
+    return order + left
+
+
 def dense_kernel(
-    parent_ref, hidden_ref, ids_ref, weight_ref, gain_ref, gate_hbm, up_hbm, down_hbm,
+    parent_ref, hidden_hbm, ids_hbm, weight_hbm, gain_hbm, gate_hbm, up_hbm, down_hbm,
     out_ref,
     *scratch,
     experts, zs,
@@ -24,6 +36,7 @@
     rows_in = [scratch.pop(0) for _ in range(gc)]
     (gate_w, up_w, down_w, gate_acc, up_acc, inner, forked_inner, share_ref, prev,
      kept, core_out, core_in, y_out, y_in, z_out, z_in,
+     hidden_ref, ids_ref, weight_ref, gain_ref,
      w_sem, g_send, g_recv, r_send, r_recv, p_sem) = scratch
     rows, width = hidden_ref.shape
     hidden_units = gate_w.shape[1]
@@ -33,13 +46,20 @@
     gw = width // gc
     rw = width // rc
     bits = zs.bit_length() - 1
+    row_bits = rows.bit_length() - 1
 
     w_copies = [
         pltpu.make_async_copy(gate_hbm.at[0], gate_w, w_sem.at[0]),
         pltpu.make_async_copy(up_hbm.at[0], up_w, w_sem.at[1]),
         pltpu.make_async_copy(down_hbm.at[0], down_w, w_sem.at[2]),
     ]
-    for copy in w_copies:
+    small_copies = [
+        pltpu.make_async_copy(hidden_hbm, hidden_ref, w_sem.at[3]),
+        pltpu.make_async_copy(ids_hbm, ids_ref, w_sem.at[4]),
+        pltpu.make_async_copy(weight_hbm, weight_ref, w_sem.at[5]),
+        pltpu.make_async_copy(gain_hbm, gain_ref, w_sem.at[6]),
+    ]
+    for copy in small_copies + w_copies:
         copy.start()
 
     me = lax.axis_index("expert")
@@ -63,6 +83,9 @@
     greeted = z_peers[1:] + [y_peer, core_peer, after, before]
     for peer in greeted:
         pl.semaphore_signal(barrier, inc=1, device_id={"expert": peer}, device_id_type=MESH)
+
+    for copy in small_copies:
+        copy.wait()
 
     own = hidden_ref[...].astype(jnp.float32)
     scale = lax.rsqrt(jnp.mean(own * own, axis=-1, keepdims=True) + 1e-06)
@@ -72,10 +95,11 @@
     parents = jnp.zeros((rows, LANES), jnp.int32)
     for r in range(rows):
         parents = jnp.where(row_no == r, parent_ref[r], parents)
-    share = weight_ref[...] / jnp.sum(weight_ref[...], axis=-1, keepdims=True)
-    ids = ids_ref[...]
+    weights = weight_ref[...].T
+    share = weights / jnp.sum(weights, axis=-1, keepdims=True)
+    ids = ids_ref[...].T
     spread = jnp.zeros((rows, LANES), jnp.float32)
-    lane_expert = lax.rem(lane, experts)
+    lane_expert = lane & (experts - 1)
     for k in range(ids.shape[1]):
         spread = spread + jnp.where(lane_expert == ids[:, k:k + 1], share[:, k:k + 1], 0.0)
     high = spread.astype(jnp.bfloat16).astype(jnp.float32)
@@ -99,11 +123,10 @@
             src_ref=src, dst_ref=dst, send_sem=send, recv_sem=recv,
             device_id={"expert": peer}, device_id_type=MESH)
 
-    def gather(k, first, count, target, number, peer):
+    def gather(k, source, target, peer):
         buf = rows_in[k]
-        return remote(buf.at[pl.ds(first * rows, count * rows), :],
-                      buf.at[pl.ds(target * rows, count * rows), :],
-                      g_send.at[k, number], g_recv.at[k, number], peer)
+        return remote(buf.at[pl.ds(source * rows, rows), :], buf.at[pl.ds(target * rows, rows), :],
+                      g_send.at[k, target], g_recv.at[k, target], peer)
 
     def go(copy):
         copy.start()
@@ -112,25 +135,20 @@
 
     z_copies, y_copies, c_copies = [], [], []
     for k in range(gc):
-        z_copies.append([go(gather(k, 0, 1, dz, dz - 1, z_peers[dz])) for dz in range(1, zs)])
-        y_copies.append([go(gather(k, 0, 1, zs, zs, y_peer))])
-        c_copies.append([go(gather(k, 0, 1, 2 * zs, zs + 1, core_peer))])
+        z_copies.append([None] + [go(gather(k, 0, dz, z_peers[dz])) for dz in range(1, zs)])
+        y_copies.append([go(gather(k, 0, zs, y_peer))])
+        c_copies.append([go(gather(k, 0, 2 * zs, core_peer))])
     before_copy = None
     tile = 256
-    for step in range(gc + 2):
-        k = step
-        if k < gc:
-            for copy in z_copies[k]:
-                copy.wait_recv()
-            y_copies[k].append(go(gather(k, 1, zs - 1, zs + 1, zs + 2, y_peer)))
-            c_copies[k].append(go(gather(k, 1, zs - 1, 2 * zs + 1, zs + 3, core_peer)))
-        k = step - 1
-        if 0 <= k < gc:
-            for copy in y_copies[k]:
-                copy.wait_recv()
-            c_copies[k].append(go(gather(k, zs, zs, 3 * zs, zs + 4, core_peer)))
-        k = step - 2
-        if 0 <= k < gc:
+    for stage, k, dz in gather_order(gc, zs):
+        if stage == "z":
+            z_copies[k][dz].wait_recv()
+            y_copies[k].append(go(gather(k, dz, zs + dz, y_peer)))
+            c_copies[k].append(go(gather(k, dz, 2 * zs + dz, core_peer)))
+        elif stage == "y":
+            y_copies[k][dz].wait_recv()
+            c_copies[k].append(go(gather(k, zs + dz, 3 * zs + dz, core_peer)))
+        else:
             for copy in c_copies[k]:
                 copy.wait_recv()
             if k == 0:
@@ -159,19 +177,19 @@
             if k == 0:
                 facts = rows_in[0][:, gw:gw + LANES].astype(jnp.float32)
                 lanes = lax.broadcasted_iota(jnp.int32, (total, LANES), 1)
-                mine = (lax.rem(lanes, experts) == me) & (lanes < 3 * experts)
+                mine = ((lanes & (experts - 1)) == me) & (lanes < 3 * experts)
                 share_ref[...] = jnp.sum(jnp.where(mine, facts, 0.0), axis=1, keepdims=True)
                 wanted = facts[:, 3 * experts:3 * experts + 1]
-                held = lax.broadcasted_iota(jnp.int32, (total, total), 1)
-                slot = lax.div(held, rows)
-                dz = lax.rem(slot, zs)
-                dy = lax.rem(lax.div(slot, zs), 2)
-                dc = lax.div(slot, 2 * zs)
+                held = lax.broadcasted_iota(jnp.int32, (8, total), 1)
+                slot = held >> row_bits
+                dz = slot & (zs - 1)
+                dy = (slot >> bits) & 1
+                dc = slot >> (bits + 1)
                 owner = dc + core - 2 * core * dc + 2 * (dy + y - 2 * y * dy)
                 for b in range(bits):
-                    bit = lax.rem(lax.div(dz, 1 << b), 2)
+                    bit = (dz >> b) & 1
                     owner = owner + (4 << b) * (bit + z_bits[b] - 2 * z_bits[b] * bit)
-                at = (owner * rows + lax.rem(held, rows)).astype(jnp.float32)
+                at = ((owner << row_bits) + (held & (rows - 1))).astype(jnp.float32)[0:1]
                 choose = jnp.where(at == wanted, 1.0, 0.0).astype(jnp.bfloat16)
 
     forked_inner[...] = jnp.dot(
@@ -196,10 +214,14 @@
     y_back = []
     for k in range(rc):
         core_copies[k].wait_recv()
-        y_out[k] = (kept[k, quarter:half] + core_in[k, quarter:half].astype(jnp.float32)
-                    ).astype(jnp.bfloat16)
-        y_back.append(go(remote(y_out.at[k], y_in.at[k],
-                                r_send.at[k, 1], r_recv.at[k, 1], y_peer)))
+        y_back.append([None] * zs)
+        for dz in reversed(range(zs)):
+            here = pl.ds(dz * rows, rows)
+            there = slice(quarter + dz * rows, quarter + (dz + 1) * rows)
+            y_out[k, here] = (kept[k, there] + core_in[k, there].astype(jnp.float32)
+                              ).astype(jnp.bfloat16)
+            y_back[k][dz] = go(remote(y_out.at[k, here], y_in.at[k, here],
+                                      r_send.at[k, 1 + dz], r_recv.at[k, 1 + dz], y_peer))
 
     before_copy.wait_recv()
     pool_no = lax.broadcasted_iota(jnp.int32, (rows, 2 * rows), 1)
@@ -208,16 +230,20 @@
 
     z_back = []
     for k in range(rc):
-        y_back[k].wait_recv()
-        summed = (kept[k, 0:quarter] + core_in[k, 0:quarter].astype(jnp.float32)
-                  + y_in[k].astype(jnp.float32))
-        kept[k, 0:rows] = summed[0:rows]
-        z_out[k] = summed[rows:quarter].astype(jnp.bfloat16)
-        z_back.append([
-            go(remote(z_out.at[k, pl.ds((dz - 1) * rows, rows), :],
-                      z_in.at[k, pl.ds((dz - 1) * rows, rows), :],
-                      r_send.at[k, 1 + dz], r_recv.at[k, 1 + dz], z_peers[dz]))
-            for dz in range(1, zs)])
+        z_back.append([None] * zs)
+        for dz in reversed(range(zs)):
+            y_back[k][dz].wait_recv()
+            block = slice(dz * rows, (dz + 1) * rows)
+            summed = (kept[k, block] + core_in[k, block].astype(jnp.float32)
+                      + y_in[k, block].astype(jnp.float32))
+            if dz == 0:
+                kept[k, block] = summed
+            else:
+                place = pl.ds((dz - 1) * rows, rows)
+                z_out[k, place] = summed.astype(jnp.bfloat16)
+                z_back[k][dz] = go(remote(
+                    z_out.at[k, place], z_in.at[k, place],
+                    r_send.at[k, zs + dz], r_recv.at[k, zs + dz], z_peers[dz]))
 
     for k in range(rc):
         columns = slice(k * rw, (k + 1) * rw)
@@ -227,7 +253,7 @@
                       preferred_element_type=jnp.float32))
         mixed = kept[k, 0:rows]
         for dz in range(1, zs):
-            z_back[k][dz - 1].wait_recv()
+            z_back[k][dz].wait_recv()
             mixed = mixed + z_in[k, (dz - 1) * rows:dz * rows].astype(jnp.float32)
         out_ref[:, columns] = (forked + mixed).astype(out_ref.dtype)
 
@@ -240,6 +266,7 @@
     experts = lax.axis_size("expert")
     zs = experts // 4
     units = w_gate.shape[2]
+    top = expert_ids.shape[1]
     total = rows * experts
     gc, rc = GATHER_CHUNKS, RETURN_CHUNKS
     gw, rw = width // gc, width // rc
@@ -249,7 +276,7 @@
     return pl.pallas_call(
         functools.partial(dense_kernel, experts=experts, zs=zs),
         out_shape=jax.ShapeDtypeStruct((rows, width), hidden.dtype),
-        in_specs=[pl.BlockSpec(memory_space=pltpu.SMEM), vmem, vmem, vmem, vmem, hbm, hbm, hbm],
+        in_specs=[pl.BlockSpec(memory_space=pltpu.SMEM)] + [hbm] * 7,
         out_specs=vmem,
         scratch_shapes=[
             pltpu.VMEM((total, gw + (LANES if k == 0 else 0)), bf16) for k in range(gc)
@@ -270,16 +297,20 @@
             pltpu.VMEM((rc, total // 4, rw), bf16),
             pltpu.VMEM((rc, total // 4 - rows, rw), bf16),
             pltpu.VMEM((rc, total // 4 - rows, rw), bf16),
-            pltpu.SemaphoreType.DMA((3,)),
-            pltpu.SemaphoreType.DMA((gc, zs + 5)),
-            pltpu.SemaphoreType.DMA((gc, zs + 5)),
-            pltpu.SemaphoreType.DMA((rc, zs + 1)),
-            pltpu.SemaphoreType.DMA((rc, zs + 1)),
+            pltpu.VMEM(hidden.shape, bf16),
+            pltpu.VMEM((top, rows), jnp.int32),
+            pltpu.VMEM((top, rows), f32),
+            pltpu.VMEM((1, width), f32),
+            pltpu.SemaphoreType.DMA((7,)),
+            pltpu.SemaphoreType.DMA((gc, 4 * zs)),
+            pltpu.SemaphoreType.DMA((gc, 4 * zs)),
+            pltpu.SemaphoreType.DMA((rc, 2 * zs)),
+            pltpu.SemaphoreType.DMA((rc, 2 * zs)),
             pltpu.SemaphoreType.DMA((2,)),
         ],
         compiler_params=pltpu.CompilerParams(
-            collective_id=0, has_side_effects=True, vmem_limit_bytes=48 * 1024 * 1024),
-    )(parent, hidden, expert_ids, route_weight, norm_gain.reshape(1, width),
+            collective_id=0, has_side_effects=True, vmem_limit_bytes=56 * 1024 * 1024),
+    )(parent, hidden, expert_ids.T, route_weight.T, norm_gain.reshape(1, width),
       w_gate, w_up, w_down)
 
 
@@ -343,7 +374,8 @@
     experts = lax.axis_size("expert")
     slots = 2 * hidden.shape[0] * others[1].shape[1]
     fits = hidden.shape[0] * experts <= min(slots, 256) and 3 * experts < LANES
-    if fits and experts >= 8 and experts & (experts - 1) == 0:
+    rows = hidden.shape[0]
+    if fits and experts >= 8 and experts & (experts - 1) == 0 and rows & (rows - 1) == 0:
         return dense(hidden, *others)
     return routed(hidden, *others)
 

time: 41.7 us -> 35.5 us (0.85)
  local copies, waits for them, and re-layouts: 6.22 us -> 1.47 us
  Pallas kernels: 35.1 us -> 33.8 us
    unnamed x11 -> x1, local copies, waits for them, and re-layouts: 6.22 us -> 1.47 us
    pallas_call x1, Pallas kernels: 35.1 us -> 33.8 us  [dense(): pl.pallas_call(functools.partial(dense_kernel, experts=experts, zs=zs), o...]
where the time goes in v2:
time: 35.5 us; the launch traced here: 35.3 us
  Pallas kernels  33.8 us (95%)
  local copies, waits for them, and re-layouts  1.47 us (4%)
    pallas_call x1, Pallas kernels, dense(): pl.pallas_call(functools.partial(dense_kernel, experts=experts, zs=zs), o...  33.8 us
    unnamed x1, local copies, waits for them, and re-layouts  1.47 us

profile of v2, /device:TPU:0, one launch (start us, length us, event | category | flops | bytes accessed | tf_op | source)
XLA Modules:
  0.0 35.3 jit_solution(15880094254937894300)
XLA Ops:
  0.0 33.8 %shard_map.82 = bf16[16,2048]{1,0:T(8,128)(2,1)} custom-call(s32[16]{0:T(128)} %parent_ref.1, bf16[16,2048]{1,0:T(8,128)(2,1)} %hidden_hbm.1, s32[8,16]{1,0:T(8,128)} %bitcast.4, f32[8,16]{1,0:T(8,128)} %bitcast.5, f32[1,2048]{1,0:T(1,128)} %bitcast.3, bf16[1,2048,768]{2,1,0:T(8,128)(2,1)} %gate_hbm.1, bf16[1,2048,768]{2,1,0:T(8,128)(2,1)} %up_hbm.1, ...), custom_call_target="tpu_custom_call" | custom-call | tf_op jit(solution)/shard_map/pallas_call | solution.py:276
  33.8 1.5 %copy.10 = bf16[16,2048]{1,0:T(8,128)(2,1)} copy(bf16[16,2048]{1,0:T(8,128)(2,1)} %shard_map.82) | data formatting | bytes 131072

commit v3 on v2

--- a/solution.py
+++ b/solution.py
@@ -157,7 +157,7 @@
             if k == gc - 1:
                 before_copy = go(remote(hidden_ref, prev, p_sem.at[0], p_sem.at[1], after))
 
-            @pl.loop(0, hidden_units // tile)
+            @pl.loop(0, hidden_units // tile, unroll=True)
             def _(t):
                 columns = pl.ds(pl.multiple_of(t * tile, tile), tile)
                 block = rows_in[k][:, 0:gw]
@@ -198,7 +198,7 @@
     core_copies = []
     for k in range(rc):
 
-        @pl.loop(0, rw // tile)
+        @pl.loop(0, rw // tile, unroll=True)
         def _(t):
             columns = pl.ds(pl.multiple_of(k * rw + t * tile, tile), tile)
             local = pl.ds(pl.multiple_of(t * tile, tile), tile)

time: 35.5 us -> 34.3 us (0.966)
  Pallas kernels: 33.8 us -> 32.7 us
    pallas_call x1, Pallas kernels: 33.8 us -> 32.7 us  [dense(): pl.pallas_call(functools.partial(dense_kernel, experts=experts, zs=zs), o...]
where the time goes in v3:
time: 34.3 us; the launch traced here: 34.1 us
  Pallas kernels  32.7 us (95%)
  local copies, waits for them, and re-layouts  1.47 us (4%)
    pallas_call x1, Pallas kernels, dense(): pl.pallas_call(functools.partial(dense_kernel, experts=experts, zs=zs), o...  32.7 us
    unnamed x1, local copies, waits for them, and re-layouts  1.47 us

profile of v3, /device:TPU:0, one launch (start us, length us, event | category | flops | bytes accessed | tf_op | source)
XLA Modules:
  0.0 34.1 jit_solution(5692589193842804370)
XLA Ops:
  0.0 32.7 %shard_map.82 = bf16[16,2048]{1,0:T(8,128)(2,1)} custom-call(s32[16]{0:T(128)} %parent_ref.1, bf16[16,2048]{1,0:T(8,128)(2,1)} %hidden_hbm.1, s32[8,16]{1,0:T(8,128)} %bitcast.4, f32[8,16]{1,0:T(8,128)} %bitcast.5, f32[1,2048]{1,0:T(1,128)} %bitcast.3, bf16[1,2048,768]{2,1,0:T(8,128)(2,1)} %gate_hbm.1, bf16[1,2048,768]{2,1,0:T(8,128)(2,1)} %up_hbm.1, ...), custom_call_target="tpu_custom_call" | custom-call | tf_op jit(solution)/shard_map/pallas_call | solution.py:276
  32.7 1.5 %copy.10 = bf16[16,2048]{1,0:T(8,128)(2,1)} copy(bf16[16,2048]{1,0:T(8,128)(2,1)} %shard_map.82) | data formatting | bytes 131072

commit v4 on v3

--- a/solution.py
+++ b/solution.py
@@ -208,12 +208,14 @@
             kept[k, :, local] = result[0:half]
             core_out[k, :, local] = result[half:total].astype(jnp.bfloat16)
 
-        core_copies.append(go(remote(core_out.at[k], core_in.at[k],
-                                     r_send.at[k, 0], r_recv.at[k, 0], core_peer)))
+        core_copies.append([
+            go(remote(core_out.at[k, pl.ds(first, quarter)], core_in.at[k, pl.ds(first, quarter)],
+                      r_send.at[k, number], r_recv.at[k, number], core_peer))
+            for first, number in ((quarter, 0), (0, 2 * zs))])
 
     y_back = []
     for k in range(rc):
-        core_copies[k].wait_recv()
+        core_copies[k][0].wait_recv()
         y_back.append([None] * zs)
         for dz in reversed(range(zs)):
             here = pl.ds(dz * rows, rows)
@@ -228,8 +230,17 @@
     pick = jnp.where(parents[:, 0:2 * rows] - (me - 1) * rows == pool_no, 1.0, 0.0)
     pick = pick.astype(jnp.bfloat16)
 
+    forked = []
+    for k in range(rc):
+        columns = slice(k * rw, (k + 1) * rw)
+        forked.append(
+            jnp.dot(pick[:, 0:rows], prev[:, columns], preferred_element_type=jnp.float32)
+            + jnp.dot(pick[:, rows:2 * rows], hidden_ref[:, columns],
+                      preferred_element_type=jnp.float32))
+
     z_back = []
     for k in range(rc):
+        core_copies[k][1].wait_recv()
         z_back.append([None] * zs)
         for dz in reversed(range(zs)):
             y_back[k][dz].wait_recv()
@@ -247,15 +258,11 @@
 
     for k in range(rc):
         columns = slice(k * rw, (k + 1) * rw)
-        forked = (
-            jnp.dot(pick[:, 0:rows], prev[:, columns], preferred_element_type=jnp.float32)
-            + jnp.dot(pick[:, rows:2 * rows], hidden_ref[:, columns],
-                      preferred_element_type=jnp.float32))
         mixed = kept[k, 0:rows]
         for dz in range(1, zs):
             z_back[k][dz].wait_recv()
             mixed = mixed + z_in[k, (dz - 1) * rows:dz * rows].astype(jnp.float32)
-        out_ref[:, columns] = (forked + mixed).astype(out_ref.dtype)
+        out_ref[:, columns] = (forked[k] + mixed).astype(out_ref.dtype)
 
     for copy in sends:
         copy.wait_send()
@@ -304,8 +311,8 @@
             pltpu.SemaphoreType.DMA((7,)),
             pltpu.SemaphoreType.DMA((gc, 4 * zs)),
             pltpu.SemaphoreType.DMA((gc, 4 * zs)),
-            pltpu.SemaphoreType.DMA((rc, 2 * zs)),
-            pltpu.SemaphoreType.DMA((rc, 2 * zs)),
+            pltpu.SemaphoreType.DMA((rc, 2 * zs + 1)),
+            pltpu.SemaphoreType.DMA((rc, 2 * zs + 1)),
             pltpu.SemaphoreType.DMA((2,)),
         ],
         compiler_params=pltpu.CompilerParams(

time: 34.3 us -> 34.2 us (level)
  no operation moved by 1% of the time
where the time goes in v4:
time: 34.2 us; the launch traced here: 34 us
  Pallas kernels  32.5 us (95%)
  local copies, waits for them, and re-layouts  1.47 us (4%)
    pallas_call x1, Pallas kernels, dense(): pl.pallas_call(functools.partial(dense_kernel, experts=experts, zs=zs), o...  32.5 us
    unnamed x1, local copies, waits for them, and re-layouts  1.47 us

profile of v4, /device:TPU:0, one launch (start us, length us, event | category | flops | bytes accessed | tf_op | source)
XLA Modules:
  0.0 34.0 jit_solution(6740861472972188769)
XLA Ops:
  0.0 32.5 %shard_map.82 = bf16[16,2048]{1,0:T(8,128)(2,1)} custom-call(s32[16]{0:T(128)} %parent_ref.1, bf16[16,2048]{1,0:T(8,128)(2,1)} %hidden_hbm.1, s32[8,16]{1,0:T(8,128)} %bitcast.4, f32[8,16]{1,0:T(8,128)} %bitcast.5, f32[1,2048]{1,0:T(1,128)} %bitcast.3, bf16[1,2048,768]{2,1,0:T(8,128)(2,1)} %gate_hbm.1, bf16[1,2048,768]{2,1,0:T(8,128)(2,1)} %up_hbm.1, ...), custom_call_target="tpu_custom_call" | custom-call | tf_op jit(solution)/shard_map/pallas_call | solution.py:283
  32.6 1.5 %copy.10 = bf16[16,2048]{1,0:T(8,128)(2,1)} copy(bf16[16,2048]{1,0:T(8,128)(2,1)} %shard_map.82) | data formatting | bytes 131072

commit v5 on v4

--- a/solution.py
+++ b/solution.py
@@ -48,6 +48,28 @@
     bits = zs.bit_length() - 1
     row_bits = rows.bit_length() - 1
 
+    me = lax.axis_index("expert")
+    core = lax.rem(me, 2)
+    y = lax.rem(lax.div(me, 2), 2)
+    z_bits = [lax.rem(lax.div(me, 4 << b), 2) for b in range(bits)]
+
+    def flipped(dz, dy, dc):
+        index = (1 - core if dc else core) + 2 * (1 - y if dy else y)
+        for b in range(bits):
+            index = index + (4 << b) * (1 - z_bits[b] if (dz >> b) & 1 else z_bits[b])
+        return index
+
+    z_peers = [flipped(dz, 0, 0) for dz in range(zs)]
+    y_peer = flipped(0, 1, 0)
+    core_peer = flipped(0, 0, 1)
+    after = lax.rem(me + 1, experts)
+    before = lax.rem(me + experts - 1, experts)
+
+    barrier = pltpu.get_barrier_semaphore()
+    greeted = z_peers[1:] + [y_peer, core_peer, after, before]
+    for peer in greeted:
+        pl.semaphore_signal(barrier, inc=1, device_id={"expert": peer}, device_id_type=MESH)
+
     w_copies = [
         pltpu.make_async_copy(gate_hbm.at[0], gate_w, w_sem.at[0]),
         pltpu.make_async_copy(up_hbm.at[0], up_w, w_sem.at[1]),
@@ -61,28 +83,6 @@
     ]
     for copy in small_copies + w_copies:
         copy.start()
-
-    me = lax.axis_index("expert")
-    core = lax.rem(me, 2)
-    y = lax.rem(lax.div(me, 2), 2)
-    z_bits = [lax.rem(lax.div(me, 4 << b), 2) for b in range(bits)]
-
-    def flipped(dz, dy, dc):
-        index = (1 - core if dc else core) + 2 * (1 - y if dy else y)
-        for b in range(bits):
-            index = index + (4 << b) * (1 - z_bits[b] if (dz >> b) & 1 else z_bits[b])
-        return index
-
-    z_peers = [flipped(dz, 0, 0) for dz in range(zs)]
-    y_peer = flipped(0, 1, 0)
-    core_peer = flipped(0, 0, 1)
-    after = lax.rem(me + 1, experts)
-    before = lax.rem(me + experts - 1, experts)
-
-    barrier = pltpu.get_barrier_semaphore()
-    greeted = z_peers[1:] + [y_peer, core_peer, after, before]
-    for peer in greeted:
-        pl.semaphore_signal(barrier, inc=1, device_id={"expert": peer}, device_id_type=MESH)
 
     for copy in small_copies:
         copy.wait()

time: 34.2 us -> 34.2 us (level)
  no operation moved by 1% of the time
where the time goes in v5:
time: 34.2 us; the launch traced here: 34 us
  Pallas kernels  32.5 us (95%)
  local copies, waits for them, and re-layouts  1.47 us (4%)
    pallas_call x1, Pallas kernels, dense(): pl.pallas_call(functools.partial(dense_kernel, experts=experts, zs=zs), o...  32.5 us
    unnamed x1, local copies, waits for them, and re-layouts  1.47 us

profile of v5, /device:TPU:0, one launch (start us, length us, event | category | flops | bytes accessed | tf_op | source)
XLA Modules:
  0.0 34.0 jit_solution(46660441045024990)
XLA Ops:
  0.0 32.5 %shard_map.82 = bf16[16,2048]{1,0:T(8,128)(2,1)} custom-call(s32[16]{0:T(128)} %parent_ref.1, bf16[16,2048]{1,0:T(8,128)(2,1)} %hidden_hbm.1, s32[8,16]{1,0:T(8,128)} %bitcast.4, f32[8,16]{1,0:T(8,128)} %bitcast.5, f32[1,2048]{1,0:T(1,128)} %bitcast.3, bf16[1,2048,768]{2,1,0:T(8,128)(2,1)} %gate_hbm.1, bf16[1,2048,768]{2,1,0:T(8,128)(2,1)} %up_hbm.1, ...), custom_call_target="tpu_custom_call" | custom-call | tf_op jit(solution)/shard_map/pallas_call | solution.py:283
  32.5 1.5 %copy.10 = bf16[16,2048]{1,0:T(8,128)(2,1)} copy(bf16[16,2048]{1,0:T(8,128)(2,1)} %shard_map.82) | data formatting | bytes 131072
